TPU v7x, 32 devices: a whole 2x2x4 slice. The times are simulated.
32 devices in a mesh: groups: 1, ado: 8 (over z, y), row: 2 (over x), sub: 2 (over core).
Axes of the slice: x: 2, y: 2, z: 4, core: 2. Of those that a mesh axis runs over, the one named last changes fastest.
Arguments:
- state: bfloat16 [768, 2, 128, 128], P(('groups', 'ado', 'sub'), None, 'row'), may hold values from -6 to 6
- hamiltonian: bfloat16 [2, 128, 128], P('groups'), may hold values from -0.5 to 0.5
- coupling: float32 [96, 128], replicated, may hold values from -3 to 3
- damping: float32 [96], replicated, may hold values from 0.05 to 1
- coef_re: float32 [96], replicated, may hold values from 0.2 to 2
- coef_im: float32 [96], replicated, may hold values from -3 to 3
- link_owner: int32 [768, 6], P(('groups', 'ado', 'sub')), may hold values from 0 to 15, all different within a row; in each aligned block of 48 rows (0 to 47, 48 to 95, ...) at most 27 rows name the same one
- link_slot: int32 [768, 6], P(('groups', 'ado', 'sub')), may hold values from 0 to 47
- link_mode: int32 [768, 6], P(('groups', 'ado', 'sub')), may hold values from 0 to 95
- link_weight: int32 [768, 6], P(('groups', 'ado', 'sub')), may hold values from 0 to 4
Outputs:
- derivative: bfloat16 [768, 2, 128, 128], P(('groups', 'ado', 'sub'), None, 'row')
Inputs may be any that keep to these rules, and one draw needn't show every extreme that they name: `link_owner`: among the links of the operators of one device (aligned blocks of 48 operators), no value is named by more than 27 links, and in every draw some value is named by exactly 27; the links of one operator name different values.
All inputs are finite; a program needn't handle non-finite values.
Results may differ from a plain program's by a relative error of at most 0.001.
Values may be sent and summed in bfloat16 or wider, within the bound.
A program may use at most 128 MiB of HBM per device.

v0:
```python
import jax
import jax.numpy as jnp
from jax import lax
from jax.sharding import PartitionSpec as P

UP = 4


def link_terms(
    rho_rows, neighbours, link_mode, link_weight, coupling, coupling_rows, damping, coef_re, coef_im
):
    modes_all = coupling.shape[0]
    select = (link_mode[:, :, None] == jnp.arange(modes_all)[None, None, :]).astype(jnp.float32)
    scale = jnp.sqrt(jnp.sqrt(coef_re * coef_re + coef_im * coef_im))
    params = jnp.stack([coef_re, coef_im, scale, damping], 1)
    picked = jnp.einsum("alk,kp->alp", select, params, precision=lax.Precision.HIGHEST)
    mode_re = picked[:, :, 0]
    mode_im = picked[:, :, 1]
    mode_scale = picked[:, :, 2]
    mode_damp = picked[:, :, 3]
    upward = (jnp.arange(link_mode.shape[1]) < UP)[None, :]
    weight_f = link_weight.astype(jnp.float32)
    root = jnp.sqrt(weight_f)
    turn = jnp.where(upward, root * mode_scale, root * mode_re / mode_scale)
    plus = jnp.where(upward, jnp.float32(0.0), root * mode_im / mode_scale)
    decay = jnp.sum(jnp.where(upward, jnp.float32(0.0), weight_f * mode_damp), 1)
    vec_rows = jnp.einsum("alk,kr->alr", select, coupling_rows, precision=lax.Precision.HIGHEST)
    vec_cols = jnp.einsum("alk,ks->als", select, coupling, precision=lax.Precision.HIGHEST)
    gap = vec_rows[:, :, :, None] - vec_cols[:, :, None, :]
    total = vec_rows[:, :, :, None] + vec_cols[:, :, None, :]
    near_re = neighbours[:, :, 0].astype(jnp.float32)
    near_im = neighbours[:, :, 1].astype(jnp.float32)
    first = turn[:, :, None, None] * gap
    second = plus[:, :, None, None] * total
    link_re = jnp.sum(first * near_im + second * near_re, 1)
    link_im = jnp.sum(second * near_im - first * near_re, 1)
    rho_re = rho_rows[:, 0].astype(jnp.float32)
    rho_im = rho_rows[:, 1].astype(jnp.float32)
    return (link_re - decay[:, None, None] * rho_re, link_im - decay[:, None, None] * rho_im)


def product_left(left, right):
    return jnp.einsum("rc,acs->ars", left, right, preferred_element_type=jnp.float32)


def product_right(left, right):
    return jnp.einsum("ars,st->art", left, right, preferred_element_type=jnp.float32)


def body(
    state,
    hamiltonian,
    coupling,
    damping,
    coef_re,
    coef_im,
    link_owner,
    link_slot,
    link_mode,
    link_weight,
):
    ados, _, rows, sites = state.shape
    links = link_owner.shape[1]
    peers = lax.axis_size(("ado", "sub"))
    capacity = max(2, min(ados, 3 * ados * links // (2 * peers)))
    row_start = lax.axis_index("row") * rows
    ham_rows = lax.dynamic_slice_in_dim(hamiltonian, row_start, rows, 1)
    coupling_rows = lax.dynamic_slice_in_dim(coupling, row_start, rows, 1)
    piece = lax.all_gather(state, "row", axis=2, tiled=True)
    part_re = product_left(ham_rows[0], piece[:, 0]) - product_left(ham_rows[1], piece[:, 1])
    part_im = product_left(ham_rows[0], piece[:, 1]) + product_left(ham_rows[1], piece[:, 0])
    owner_flat = link_owner.reshape(-1)
    slot_flat = link_slot.reshape(-1)
    onehot = (owner_flat[:, None] == jnp.arange(peers, dtype=jnp.int32)[None, :]).astype(jnp.int32)
    rank_flat = jnp.sum((jnp.cumsum(onehot, 0) - 1) * onehot, 1)
    outgoing = jnp.zeros((peers, capacity), jnp.int32).at[owner_flat, rank_flat].set(slot_flat)
    wanted = lax.all_to_all(outgoing, ("ado", "sub"), split_axis=0, concat_axis=0, tiled=True)
    sending = jnp.take(state, wanted.reshape(-1), axis=0).reshape(peers, capacity, 2, rows, sites)
    arrived = lax.all_to_all(sending, ("ado", "sub"), split_axis=0, concat_axis=0, tiled=True)
    arrived = arrived.reshape(peers * capacity, 2, rows, sites)
    neighbours = jnp.take(arrived, owner_flat * capacity + rank_flat, axis=0).reshape(
        ados, links, 2, rows, sites
    )
    right_re = product_right(state[:, 0], hamiltonian[0]) - product_right(
        state[:, 1], hamiltonian[1]
    )
    right_im = product_right(state[:, 0], hamiltonian[1]) + product_right(
        state[:, 1], hamiltonian[0]
    )
    link_re, link_im = link_terms(
        state,
        neighbours,
        link_mode,
        link_weight,
        coupling,
        coupling_rows,
        damping,
        coef_re,
        coef_im,
    )
    out_re = part_im - right_im + link_re
    out_im = right_re - part_re + link_im
    return jnp.stack([out_re, out_im], 1).astype(jnp.bfloat16)


def solution(mesh):
    placed = (
        P(("groups", "ado", "sub"), None, "row", None),
        P("groups", None, None),
        P(),
        P(),
        P(),
        P(),
        P(("groups", "ado", "sub"), None),
        P(("groups", "ado", "sub"), None),
        P(("groups", "ado", "sub"), None),
        P(("groups", "ado", "sub"), None),
    )
    return jax.shard_map(
        body,
        mesh=mesh,
        in_specs=placed,
        out_specs=P(("groups", "ado", "sub"), None, "row", None),
        check_vma=False,
    )
```

profile of v0, /device:TPU:13, one launch (start us, length us, event | category | flops | bytes accessed | tf_op | source)
XLA Modules:
  0.0 420.1 jit_solution(5094870857272117143)
XLA Ops:
  6.5 0.8 copy.75
  7.6 0.9 reduce-window.6
  8.8 0.8 copy.81
  9.8 15.2 %scatter_fusion = s32[16,27]{1,0:T(8,128)S(1)} fusion(s32[16,27]{1,0:T(8,128)S(1)} %broadcast_in_dim.65, s32[288]{0:T(512)S(1)} %get-tuple-element.8, s32[288]{0:T(512)S(1)} %reshape.191), kind=kCustom, calls=%fused_computation.2 | custom fusion | bytes 5760 | tf_op jit(solution)/shard_map/scatter | solution.py:76
  25.0 10.2 %all_to_all.14 = s32[16,1,27]{2,1,0:T(1,128)S(1)} all-to-all(s32[16,1,27]{2,1,0:T(1,128)S(1)} %bitcast.150), channel_id=1, replica_groups=mesh['groups'=1,'ado'=8,'row'=2,'sub'=2] {'ado','sub'}, dimensions={0} | all-to-all | bytes 3456 | tf_op jit(solution)/shard_map/all_to_all | solution.py:77
  35.6 0.7 reduce.9
  36.4 12.9 %gather_fusion = bf16[432,2,64,128]{3,2,1,0:T(8,128)(2,1)} fusion(bf16[48,2,64,128]{3,2,1,0:T(8,128)(2,1)S(1)} %copy-done.2, s32[1024]{0:T(1024)S(1)} %pad_clamp_fusion.1), kind=kCustom, calls=%fused_computation | custom fusion | bytes 28313280 | tf_op jit(solution)/shard_map/jit(_take)/gather | solution.py:78
  49.4 12.9 %broadcast_select_fusion = bf16[16,27,2,64,128]{4,3,2,1,0:T(8,128)(2,1)} fusion(bf16[16,27,2,64,128]{4,3,2,1,0:T(8,128)(2,1)} %bitcast.151, pred[16,27]{1,0:T(8,128)(4,1)S(1)} %compare_and_fusion), kind=kLoop, calls=%fused_computation.3 | loop fusion | flops 7077888 | bytes 28311984 | tf_op jit(solution)/shard_map/jit(_take)/select_n | solution.py:78
  62.2 7.7 %all-to-all-start.1 = ((bf16[16,27,2,64,128]{4,3,2,1,0:T(8,128)(2,1)}), bf16[16,27,2,64,128]{4,3,2,1,0:T(8,128)(2,1)}, u32[]{:S(2)}, u32[]{:S(2)}) async-start(bf16[16,27,2,64,128]{4,3,2,1,0:T(8,128)(2,1)} %broadcast_select_fusion), calls=%async_computation.1 | async-start | bytes 28311552 | tf_op jit(solution)/shard_map/all_to_all | solution.py:79
  70.1 1.3 copy.66
  73.6 0.7 copy.74
  74.4 1.5 fusion.13
  75.9 1.5 fusion.15
  77.7 1.5 fusion.14
  79.2 38.6 %all-gather.2.cloned.1.call-done = bf16[48,2,128,128]{3,2,0,1:T(8,128)(2,1)} async-done(((bf16[48,2,64,128]{3,2,0,1:T(8,128)(2,1)}), bf16[48,2,128,128]{3,2,0,1:T(8,128)(2,1)}) %all-gather.2.cloned.1.call-update) | async-done | bytes 3145744 | tf_op jit(solution)/shard_map/all_gather | solution.py:69
  117.9 3.1 fusion.8
  121.0 1.5 fusion.9
  122.5 253.4 %all-to-all-done.1 = bf16[16,27,2,64,128]{4,3,2,1,0:T(8,128)(2,1)} async-done(((bf16[16,27,2,64,128]{4,3,2,1,0:T(8,128)(2,1)}), bf16[16,27,2,64,128]{4,3,2,1,0:T(8,128)(2,1)}, u32[]{:S(2)}, u32[]{:S(2)}) %all-to-all-start.1) | async-done | bytes 14155808 | tf_op jit(solution)/shard_map/all_to_all | solution.py:79
  375.8 15.4 %gather_fusion.1 = bf16[288,2,64,128]{3,2,1,0:T(8,128)(2,1)} fusion(bf16[432,2,64,128]{3,2,1,0:T(8,128)(2,1)} %bitcast.28, s32[1024]{0:T(1024)S(1)} %pad_clamp_fusion), kind=kCustom, calls=%fused_computation.1 | custom fusion | bytes 18875520 | tf_op jit(solution)/shard_map/jit(_take)/gather | solution.py:81
  391.2 8.2 %broadcast_select_fusion.1 = bf16[48,6,2,64,128]{4,3,2,1,0:T(8,128)(2,1)} fusion(bf16[48,6,2,64,128]{4,3,2,1,0:T(8,128)(2,1)} %bitcast.152, pred[48,6]{1,0:T(8,128)(4,1)S(1)} %copy.79), kind=kLoop, calls=%fused_computation.14 | loop fusion | flops 4718592 | bytes 18874656 | tf_op jit(solution)/shard_map/jit(_take)/select_n | solution.py:81
  399.5 9.5 %fusion.1 = (f32[48,64,128]{2,1,0:T(8,128)S(1)}, f32[48,64,128]{2,1,0:T(8,128)S(1)}) fusion(f32[48,6]{1,0:T(8,128)S(1)} %copy.85, f32[48,6,128]{2,1,0:T(8,128)} %copy.74, f32[48,6,64]{2,1,0:T(8,128)S(1)} %copy.73, f32[48,6]{1,0:T(8,128)S(1)} %copy.71, bf16[48,6,2,64,128]{4,3,2,1,0:T(8,128)(2,1)} %broadcast_select_fusion.1), kind=kLoop, calls=%fused_computation.9 | loop fusion | flops 32243712 | bytes 12806400 | tf_op jit(solution)/shard_map/reduce_sum | solution.py:35
  409.0 0.8 fusion.10
  410.9 0.9 fusion.11
  411.9 1.3 copy.86
  (69 shorter events, 5.3 us)
Async XLA Ops:
  6.5 66.5 %copy-start = (f32[96,128]{1,0:T(8,128)S(1)}, f32[96,128]{1,0:T(8,128)}, u32[]{:S(2)}) copy-start(f32[96,128]{1,0:T(8,128)} %param.12) | copy-start | bytes 147460
  9.8 26.7 %copy-start.2 = (bf16[48,2,64,128]{3,2,1,0:T(8,128)(2,1)S(1)}, bf16[48,2,64,128]{3,2,1,0:T(8,128)(2,1)}, u32[]{:S(2)}) copy-start(bf16[48,2,64,128]{3,2,1,0:T(8,128)(2,1)} %param.10) | copy-start | bytes 4718596
  62.2 313.6 %all-to-all-start.1 = ((bf16[16,27,2,64,128]{4,3,2,1,0:T(8,128)(2,1)}), bf16[16,27,2,64,128]{4,3,2,1,0:T(8,128)(2,1)}, u32[]{:S(2)}, u32[]{:S(2)}) async-start(bf16[16,27,2,64,128]{4,3,2,1,0:T(8,128)(2,1)} %broadcast_select_fusion), calls=%async_computation.1 | async-start | bytes 28311552 | tf_op jit(solution)/shard_map/all_to_all | solution.py:79
  69.9 48.0 %all-gather.2.cloned.1.call-start = ((), (), s32[]{:S(2)}) async-start(), calls=%async_computation.2 | async-start | bytes 4718592 | tf_op jit(solution)/shard_map/all_gather | solution.py:69
  71.4 0.7 copy-start.12
  71.4 0.8 copy-start.15
  71.4 0.8 copy-start.16
  71.4 0.8 copy-start.11
  71.4 0.9 copy-start.14
  71.4 1.3 copy-start.13
  71.4 2.9 copy-start.10
  117.9 3.1 copy-start.3
  399.5 9.5 %copy-start.4 = (bf16[48,2,128,128]{3,2,0,1:T(8,128)(2,1)S(1)}, bf16[48,2,128,128]{3,2,0,1:T(8,128)(2,1)}, u32[]{:S(2)}) copy-start(bf16[48,2,128,128]{3,2,0,1:T(8,128)(2,1)} %all-gather.2.cloned.1.call-done) | copy-start | bytes 9437188
  399.5 9.5 %copy-start.7 = (f32[48,64,128]{2,1,0:T(8,128)S(1)}, f32[48,64,128]{2,1,0:T(8,128)}, u32[]{:S(2)}) copy-start(f32[48,64,128]{2,1,0:T(8,128)} %fusion.13) | copy-start | bytes 4718596
  399.5 9.5 %copy-start.8 = (f32[48,64,128]{2,1,0:T(8,128)S(1)}, f32[48,64,128]{2,1,0:T(8,128)}, u32[]{:S(2)}) copy-start(f32[48,64,128]{2,1,0:T(8,128)} %fusion.15) | copy-start | bytes 4718596
  399.5 9.5 %copy-start.9 = (f32[64,48,128]{2,0,1:T(8,128)S(1)}, f32[64,48,128]{2,0,1:T(8,128)}, u32[]{:S(2)}) copy-start(f32[64,48,128]{2,0,1:T(8,128)} %fusion.8) | copy-start | bytes 4718596
  409.0 1.4 copy-start.5
  409.0 1.9 copy-start.6
  411.8 1.5 copy-start.1
Sparse Core Ops, SparseCore 0:
  72.3 45.5 all-gather.1
where the time goes:
time: 421 us; the launch traced here: 420 us
  waiting for transfers between devices  292 us (69%)
  local copies, waits for them, and re-layouts  51.6 us (12%)
  other arithmetic  32.6 us (8%)
  between operations  13.7 us (3%)
  matrix products  12.1 us (3%)
  blocking collectives  10.2 us (2%)
  starting transfers between devices  7.89 us (2%)
    all_to_all x1, waiting for transfers between devices, body(): lax.all_to_all(sending, ('ado', 'sub'), split_axis=0, concat_axis=0, tile...  253 us
    all_gather x1, waiting for transfers between devices, body(): piece = lax.all_gather(state, 'row', axis=2, tiled=True)  38.6 us
    gather x1, local copies, waits for them, and re-layouts, body(): jnp.take(arrived, owner_flat * capacity + rank_flat, axis=0)  15.4 us
    scatter x1, local copies, waits for them, and re-layouts, body(): jnp.zeros((peers, capacity), jnp.int32).at[owner_flat, rank_flat]  15.2 us
    gather x1, local copies, waits for them, and re-layouts, body(): jnp.take(state, wanted.reshape(-1), axis=0)  12.9 us
    select_n x2, other arithmetic, body(): jnp.take(state, wanted.reshape(-1), axis=0)  12.9 us
    all_to_all x1, blocking collectives, body(): lax.all_to_all(outgoing, ('ado', 'sub'), split_axis=0, concat_axis=0, til...  10.2 us
    reduce_sum x1, other arithmetic, link_terms(): link_re = jnp.sum(first * near_im + second * near_re, 1)  9.49 us
  transfers between devices with their start and end apart: 2, of which 2 were waited for; matrix products, arithmetic and copies ran while one was open for 3% of the time, Pallas kernels for 0%

commit v1 on v0

--- a/solution.py
+++ b/solution.py
@@ -1,6 +1,8 @@
 import jax
 import jax.numpy as jnp
 from jax import lax
+from jax.experimental import pallas as pl
+from jax.experimental.pallas import tpu as pltpu
 from jax.sharding import PartitionSpec as P
 
 UP = 4
@@ -103,7 +105,318 @@
     return jnp.stack([out_re, out_im], 1).astype(jnp.bfloat16)
 
 
+MESH = pl.DeviceIdType.MESH
+CHUNKS = 4
+IN, OUT, SIDE, PAIR = 0, 1, 2, 3
+
+END_IN = [
+    (1, 0, 0, (SIDE,)),
+    (1, 0, 1, ()),
+    (2, 0, 0, (SIDE,)),
+    (2, 0, 1, (SIDE,)),
+    (3, 0, 0, (SIDE,)),
+    (3, 0, 1, (SIDE,)),
+    (1, 1, 1, ()),
+]
+END_SIDE = [
+    (0, 1, 0, (IN,)),
+    (0, 1, 1, (IN,)),
+    (1, 1, 0, ()),
+    (2, 1, 0, ()),
+    (2, 1, 1, ()),
+    (3, 1, 0, ()),
+    (3, 1, 1, ()),
+]
+MID_IN = [
+    (2, 0, 0, (OUT, SIDE)),
+    (2, 0, 1, (OUT, SIDE)),
+    (3, 0, 0, (OUT,)),
+    (3, 0, 1, (OUT,)),
+    (3, 1, 0, ()),
+    (3, 1, 1, ()),
+]
+MID_OUT = [(0, 0, 0, (IN,)), (0, 0, 1, (IN,)), (0, 1, 0, (IN,)), (0, 1, 1, (IN,))]
+MID_SIDE = [(1, 1, 0, ()), (1, 1, 1, ()), (2, 1, 0, ()), (2, 1, 1, ())]
+MID_LATE = (1, 1, 1, (OUT,))
+
+
+def root_of(w):
+    low = jnp.where(w == 1, jnp.float32(1.0), jnp.float32(0.0))
+    low = jnp.where(w == 2, jnp.float32(2.0**0.5), low)
+    low = jnp.where(w == 3, jnp.float32(3.0**0.5), low)
+    return jnp.where(w == 4, jnp.float32(2.0), low)
+
+
+def kernel(
+    state,
+    ham,
+    coupling,
+    damping,
+    coef_re,
+    coef_im,
+    owner,
+    slot,
+    mode,
+    weight,
+    out,
+    held,
+    full,
+    acc,
+    up_turn,
+    down_turn,
+    down_plus,
+    right_mat,
+    left_mat,
+    send,
+    recv,
+    local,
+):
+    ados, _, rows, sites = state.shape
+    links = owner.shape[1]
+    modes = coupling.shape[0]
+    a, c, r = lax.axis_index("ado"), lax.axis_index("sub"), lax.axis_index("row")
+    z, y = a // 2, a % 2
+    low = z < 2
+    inward = jnp.where(low, 1, -1)
+    place = jnp.where(low, z, 3 - z)
+    at_end, at_mid = place == 0, place == 1
+    to = {
+        IN: {"ado": (z + inward) * 2 + y},
+        OUT: {"ado": (z - inward) * 2 + y},
+        SIDE: {"ado": z * 2 + 1 - y},
+        PAIR: {"sub": 1 - c},
+    }
+    size = ados // CHUNKS
+    half_chunks = CHUNKS // 2
+
+    def ado_of(p, other):
+        return jnp.where(low, p, 3 - p) * 2 + (1 - y if other else y)
+
+    def copy(way, index, chunk, own=False):
+        piece = pl.ds(chunk * size, size)
+        block = index * 2 + c
+        return pltpu.make_async_remote_copy(
+            src_ref=state.at[piece] if own else held.at[block, piece],
+            dst_ref=held.at[block, piece],
+            send_sem=send.at[way, index, chunk],
+            recv_sem=recv.at[block, chunk],
+            device_id=to[way],
+            device_id_type=MESH,
+        )
+
+    def from_pair(index, chunk):
+        piece = pl.ds(chunk * size, size)
+        block = index * 2 + 1 - c
+        return pltpu.make_async_remote_copy(
+            src_ref=held.at[block, piece],
+            dst_ref=held.at[block, piece],
+            send_sem=send.at[PAIR, index, chunk],
+            recv_sem=recv.at[block, chunk],
+            device_id=to[PAIR],
+            device_id_type=MESH,
+        )
+
+    mine = pl.ds(pl.multiple_of(r * rows, rows), rows)
+    row_copy = pltpu.make_async_remote_copy(
+        src_ref=state,
+        dst_ref=full.at[:, :, mine],
+        send_sem=local.at[0],
+        recv_sem=local.at[1],
+        device_id={"row": 1 - r},
+        device_id_type=MESH,
+    )
+    own_held = pltpu.make_async_copy(state, held.at[a * 2 + c], local.at[2])
+    own_full = pltpu.make_async_copy(state, full.at[:, :, mine], local.at[3])
+
+    barrier = pltpu.get_barrier_semaphore()
+    for target in (to[IN], to[SIDE], to[PAIR], {"row": 1 - r}):
+        pl.semaphore_signal(barrier, inc=1, device_id=target, device_id_type=MESH)
+
+    @pl.when(at_mid)
+    def _():
+        pl.semaphore_signal(barrier, inc=1, device_id=to[OUT], device_id_type=MESH)
+        pl.semaphore_wait(barrier, 5)
+
+    @pl.when(at_end)
+    def _():
+        pl.semaphore_wait(barrier, 4)
+
+    def own_sends(ways, act):
+        for k in range(CHUNKS):
+            for way in ways:
+                act(copy(way, a, k, own=True))
+
+    start = lambda d: d.start()
+    done = lambda d: d.wait_send()
+
+    own_sends((IN, SIDE), start)
+
+    @pl.when(at_mid)
+    def _():
+        own_sends((OUT,), start)
+
+    row_copy.start()
+    own_held.start()
+    own_full.start()
+    own_sends((PAIR,), start)
+
+    right_mat[:sites, :sites] = -ham[1]
+    right_mat[:sites, sites:] = ham[0]
+    right_mat[sites:, :sites] = -ham[0]
+    right_mat[sites:, sites:] = -ham[1]
+    left_mat[:rows, :sites] = ham[1, mine, :]
+    left_mat[:rows, sites:] = ham[0, mine, :]
+    left_mat[rows:, :sites] = -ham[0, mine, :]
+    left_mat[rows:, sites:] = ham[1, mine, :]
+
+    def table(k, carry):
+        cols = coupling[pl.ds(k, 1), :]
+        turned = jnp.transpose(jnp.broadcast_to(cols, (sites, sites)))
+        here = jnp.where(r == 0, turned[:rows], turned[rows:])
+        re = jnp.full((8, sites), coef_re[k])
+        im = jnp.full((8, sites), coef_im[k])
+        scale = jnp.sqrt(jnp.sqrt(re * re + im * im))
+        gap = (here - cols).reshape(rows // 8, 8, sites)
+        total = (here + cols).reshape(rows // 8, 8, sites)
+        up_turn[k] = (scale * gap).reshape(rows, sites)
+        down_turn[k] = (re / scale * gap).reshape(rows, sites)
+        down_plus[k] = (im / scale * total).reshape(rows, sites)
+        return carry
+
+    lax.fori_loop(0, modes, table, 0)
+
+    def product(n, carry):
+        both = jnp.concatenate([full[n, 0], full[n, 1]], axis=0)
+        left = jnp.dot(left_mat[...], both, preferred_element_type=jnp.float32)
+        own_re, own_im = full[n, 0, mine, :], full[n, 1, mine, :]
+        right = jnp.dot(
+            jnp.concatenate([own_re, own_im], axis=1),
+            right_mat[...],
+            preferred_element_type=jnp.float32,
+        )
+        decay = jnp.float32(0.0)
+        for j in range(UP, links):
+            decay = decay + weight[n, j].astype(jnp.float32) * damping[mode[n, j]]
+        acc[n, 0] = left[:rows] + right[:, :sites] - decay * own_re.astype(jnp.float32)
+        acc[n, 1] = left[rows:] + right[:, sites:] - decay * own_im.astype(jnp.float32)
+        return carry
+
+    def products(part):
+        third = ados // 3
+        if part == 0:
+            row_copy.wait_recv()
+            own_full.wait()
+        lax.fori_loop(part * third, (part + 1) * third, product, 0)
+
+    def chunks_of(half):
+        return range(half * half_chunks, (half + 1) * half_chunks)
+
+    def run(streams, late):
+        for s in range(max(len(stream) for stream in streams)):
+            for i in range(half_chunks):
+                for stream in streams:
+                    if s < len(stream):
+                        p, other, half, ways = stream[s]
+                        index, k = ado_of(p, other), half * half_chunks + i
+                        copy(PAIR, index, k).wait_recv()
+                        for way in ways + (PAIR,):
+                            copy(way, index, k).start()
+            if s == 4 and late is not None:
+                for k in chunks_of(late[2]):
+                    for way in late[3]:
+                        copy(way, ado_of(late[0], late[1]), k).start()
+            if 2 <= s <= 4:
+                products(s - 2)
+
+    def drain(streams, late):
+        for stream in list(streams) + ([[late]] if late is not None else []):
+            for p, other, half, ways in stream:
+                for k in chunks_of(half):
+                    for way in ways + (() if stream == [late] else (PAIR,)):
+                        copy(way, ado_of(p, other), k).wait_send()
+
+    @pl.when(at_end)
+    def _():
+        run((END_IN, END_SIDE), None)
+
+    @pl.when(at_mid)
+    def _():
+        run((MID_IN, MID_OUT, MID_SIDE), MID_LATE)
+
+    own_held.wait()
+    for index in range(8):
+        for k in range(CHUNKS):
+            from_pair(index, k).wait_recv()
+
+    def gather(n, carry):
+        sum_re, sum_im = acc[n, 0], acc[n, 1]
+        for j in range(links):
+            o, s, k = owner[n, j], slot[n, j], mode[n, j]
+            root = root_of(weight[n, j])
+            near = held[o, s].astype(jnp.float32)
+            near_re, near_im = near[0], near[1]
+            first = root * (up_turn[k] if j < UP else down_turn[k])
+            sum_re = sum_re + first * near_im
+            sum_im = sum_im - first * near_re
+            if j >= UP:
+                second = root * down_plus[k]
+                sum_re = sum_re + second * near_re
+                sum_im = sum_im + second * near_im
+        out[n, 0] = sum_re.astype(jnp.bfloat16)
+        out[n, 1] = sum_im.astype(jnp.bfloat16)
+        return carry
+
+    lax.fori_loop(0, ados, gather, 0)
+
+    own_sends((IN, SIDE, PAIR), done)
+    row_copy.wait_send()
+
+    @pl.when(at_mid)
+    def _():
+        own_sends((OUT,), done)
+        drain((MID_IN, MID_OUT, MID_SIDE), MID_LATE)
+
+    @pl.when(at_end)
+    def _():
+        drain((END_IN, END_SIDE), None)
+
+
+def fused(*args):
+    state, coupling = args[0], args[2]
+    ados, _, rows, sites = state.shape
+    modes = coupling.shape[0]
+    peers = lax.axis_size(("ado", "sub"))
+    chips = peers // 2
+    vmem = pl.BlockSpec(memory_space=pltpu.VMEM)
+    smem = pl.BlockSpec(memory_space=pltpu.SMEM)
+    return pl.pallas_call(
+        kernel,
+        out_shape=jax.ShapeDtypeStruct(state.shape, jnp.bfloat16),
+        in_specs=[pl.BlockSpec(memory_space=pl.ANY), vmem, vmem] + [smem] * 7,
+        out_specs=vmem,
+        scratch_shapes=[
+            pltpu.VMEM((peers, ados, 2, rows, sites), jnp.bfloat16),
+            pltpu.VMEM((ados, 2, 2 * rows, sites), jnp.bfloat16),
+            pltpu.VMEM((ados, 2, rows, sites), jnp.float32),
+            pltpu.VMEM((modes, rows, sites), jnp.float32),
+            pltpu.VMEM((modes, rows, sites), jnp.float32),
+            pltpu.VMEM((modes, rows, sites), jnp.float32),
+            pltpu.VMEM((2 * sites, 2 * sites), jnp.bfloat16),
+            pltpu.VMEM((2 * rows, 2 * sites), jnp.bfloat16),
+            pltpu.SemaphoreType.DMA((4, chips, CHUNKS)),
+            pltpu.SemaphoreType.DMA((peers, CHUNKS)),
+            pltpu.SemaphoreType.DMA((4,)),
+        ],
+        compiler_params=pltpu.CompilerParams(
+            collective_id=0, has_side_effects=True, vmem_limit_bytes=56 * 1024 * 1024
+        ),
+    )(*args)
+
+
 def solution(mesh):
+    grid = mesh.shape["groups"] == 1 and mesh.shape["ado"] == 8
+    grid = grid and mesh.shape["row"] == 2 and mesh.shape["sub"] == 2
+    step = fused if grid else body
     placed = (
         P(("groups", "ado", "sub"), None, "row", None),
         P("groups", None, None),
@@ -117,7 +430,7 @@
         P(("groups", "ado", "sub"), None),
     )
     return jax.shard_map(
-        body,
+        step,
         mesh=mesh,
         in_specs=placed,
         out_specs=P(("groups", "ado", "sub"), None, "row", None),

time: 421 us -> 143 us (0.34)
  the two profiles are of different devices: /device:TPU:13 before, /device:TPU:1 now
where the time goes in v1:
time: 143 us; the launch traced here: 142 us
  Pallas kernels  134 us (94%)
  local copies, waits for them, and re-layouts  8.25 us (6%)
    pallas_call x1, Pallas kernels, fused(): pl.pallas_call(kernel, out_shape=jax.ShapeDtypeStruct(state.shape, jnp.bf...  134 us
    unnamed x5, local copies, waits for them, and re-layouts  8.25 us

profile of v1, /device:TPU:1, one launch (start us, length us, event | category | flops | bytes accessed | tf_op | source)
XLA Modules:
  0.0 142.2 jit_solution(15430062305381252121)
XLA Ops:
  0.0 1.4 copy.11.owner
  1.4 1.4 copy.12.slot
  2.7 1.4 copy.13.mode
  4.1 1.4 copy.14.weight
  5.5 134.0 %shard_map.100 = bf16[48,2,64,128]{3,2,1,0:T(8,128)(2,1)} custom-call(bf16[48,2,64,128]{3,2,1,0:T(8,128)(2,1)} %state.1, bf16[2,128,128]{2,1,0:T(8,128)(2,1)} %ham.1, f32[96,128]{1,0:T(8,128)} %coupling.1, f32[96]{0:T(128)} %damping.1, f32[96]{0:T(128)} %coef_re.1, f32[96]{0:T(128)} %coef_im.1, s32[48,6]{1,0:T(8,128)} %copy.11.owner, s32[48,6]{1,0:T(8,128)} %copy.12.slot, ...), custom_call_target="tpu_custom_call" | custom-call | tf_op jit(solution)/shard_map/pallas_call | solution.py:392
  139.5 2.8 %copy.16 = bf16[48,2,64,128]{3,2,1,0:T(8,128)(2,1)} copy(bf16[48,2,64,128]{3,2,1,0:T(8,128)(2,1)} %shard_map.100) | data formatting | bytes 3145728
